TPU v7x, 128 devices: a whole 4x4x4 slice. The times are simulated.
128 devices in a mesh: aux: 4 (over x), pair: 32 (over z, y, core).
Axes of the slice: x: 4, y: 4, z: 4, core: 2. Of those that a mesh axis runs over, the one named last changes fastest.
Arguments:
- three_index: bfloat16 [512, 256, 2048], P('pair', None, 'aux'), may hold values from -0.875 to 0.875
- fock_diag: float32 [512], replicated, may hold values from -1.2 to -0.3
- pair_occ: int32 [992, 2], P('pair'), may hold values from 0 to 511, as said below
- pno_count: int32 [992], P('pair'), may hold values from 32 to 128
- pno_energy: float32 [992, 128], P('pair'), may hold values from 0.3 to 3
- pno_coef: bfloat16 [992, 2, 256, 128], P('pair'), may hold values from -0.375 to 0.375
Outputs:
- pair_energy: float32 [992], P('pair')
- grad_ints: float32 [512, 256, 2048], P('pair', None, 'aux')
Inputs may be any that keep to these rules, and one draw needn't show every extreme that they name: `pair_occ`: orbital o belongs to the block o // 16. Among the 62 orbitals named by the pairs of one aligned block of 31 rows, at most 2 belong to any one orbital block, and one orbital block receives exactly 2 from every such row block; i may equal j.
All inputs are finite; a program needn't handle non-finite values.
Results may differ from a plain program's by a relative error of at most 0.0061.
Values may be sent and summed in bfloat16 or wider, within the bound.
A program may use at most 128 MiB of HBM per device.

v0:
```python
import jax
import jax.numpy as jnp
from jax import lax
from jax.sharding import PartitionSpec as P


def local(three_index, fock_diag, pair_occ, pno_count, pno_energy, pno_coef):
    groups = lax.axis_size("pair")
    occ_dev = three_index.shape[0]
    width_dom = three_index.shape[1]
    width_aux = three_index.shape[2]
    pair_dev = pair_occ.shape[0]
    width_pno = pno_coef.shape[3]
    halves = 2 * pair_dev
    capacity = max(2, halves // groups + 1)
    slots = groups * capacity
    occ_flat = pair_occ.reshape(halves)
    owner_of = occ_flat // occ_dev
    local_index = occ_flat % occ_dev
    owner_hot = (owner_of[:, None] == jnp.arange(groups, dtype=jnp.int32)[None, :]).astype(
        jnp.int32
    )
    before = jnp.cumsum(owner_hot, axis=0) - owner_hot
    rank_in = jnp.sum(before * owner_hot, axis=1)
    slot_of = owner_of * capacity + rank_in
    request = jnp.zeros((slots,), jnp.int32).at[slot_of].set(local_index + 1)
    arrived = lax.all_to_all(
        request.reshape(groups, capacity), "pair", split_axis=0, concat_axis=0, tiled=True
    ).reshape(slots)
    is_live = arrived > 0
    row_index = jnp.maximum(arrived - 1, 0)
    selected = jnp.take(three_index, row_index, axis=0)
    selected = jnp.where(is_live[:, None, None], selected, jnp.zeros_like(selected))
    coef_half = pno_coef.reshape(halves, width_dom, width_pno)
    rows_back = lax.all_to_all(
        selected.reshape(groups, capacity, width_dom, width_aux),
        "pair",
        split_axis=0,
        concat_axis=0,
        tiled=True,
    )
    mine = jnp.take(rows_back.reshape(slots, width_dom, width_aux), slot_of, axis=0)
    projected = jnp.einsum(
        "hdp,hdq->hpq", coef_half, mine, preferred_element_type=jnp.float32
    ).astype(jnp.bfloat16)
    paired = projected.reshape(pair_dev, 2, width_pno, width_aux)
    rows_i = paired[:, 0]
    rows_j = paired[:, 1]
    partial_sum = jnp.einsum("kpq,krq->kpr", rows_i, rows_j, preferred_element_type=jnp.float32)
    coupling = lax.psum(partial_sum, "aux")
    fock_i = jnp.take(fock_diag, pair_occ[:, 0])
    fock_j = jnp.take(fock_diag, pair_occ[:, 1])
    denom = pno_energy[:, :, None] + pno_energy[:, None, :] - (fock_i + fock_j)[:, None, None]
    in_pno = jnp.arange(width_pno, dtype=jnp.int32)[None, :] < pno_count[:, None]
    both_in = in_pno[:, :, None] & in_pno[:, None, :]
    amplitude = jnp.where(both_in, -coupling / denom, jnp.float32(0.0))
    mixed = 2.0 * amplitude - jnp.swapaxes(amplitude, 1, 2)
    energy = jnp.sum(coupling * mixed, axis=(1, 2)) / (width_pno * width_pno)
    weights = mixed.astype(jnp.bfloat16)
    gamma_i = jnp.einsum(
        "kab,kbq->kaq", weights, rows_j, preferred_element_type=jnp.float32
    ).astype(jnp.bfloat16)
    gamma_j = jnp.einsum(
        "kba,kbq->kaq", weights, rows_i, preferred_element_type=jnp.float32
    ).astype(jnp.bfloat16)
    gamma = jnp.stack([gamma_i, gamma_j], axis=1).reshape(halves, width_pno, width_aux)
    dom_terms = jnp.einsum(
        "hdp,hpq->hdq", coef_half, gamma, preferred_element_type=jnp.float32
    ).astype(jnp.bfloat16)
    term_send = jnp.zeros((slots, width_dom, width_aux), jnp.bfloat16).at[slot_of].set(dom_terms)
    terms = lax.all_to_all(
        term_send.reshape(groups, capacity, width_dom, width_aux),
        "pair",
        split_axis=0,
        concat_axis=0,
        tiled=True,
    )
    terms = terms.reshape(slots, width_dom, width_aux)
    occ_hot = (row_index[None, :] == jnp.arange(occ_dev, dtype=jnp.int32)[:, None]) & is_live[
        None, :
    ]
    grad = jnp.dot(
        occ_hot.astype(jnp.bfloat16),
        terms.reshape(slots, width_dom * width_aux),
        preferred_element_type=jnp.float32,
    )
    return (energy, grad.reshape(occ_dev, width_dom, width_aux))


def solution(mesh):
    placed = (
        P("pair", None, "aux"),
        P(),
        P("pair", None),
        P("pair"),
        P("pair", None),
        P("pair", None, None, None),
    )
    return jax.shard_map(
        local,
        mesh=mesh,
        in_specs=placed,
        out_specs=(P("pair"), P("pair", None, "aux")),
        check_vma=False,
    )
```

profile of v0, /device:TPU:0, one launch (start us, length us, event | category | flops | bytes accessed | tf_op | source)
XLA Modules:
  0.0 715.7 jit_solution(3268946440946229828)
XLA Ops:
  7.2 0.0 copy-start
  7.2 0.8 copy.56
  8.0 0.1 reshape.245
  8.1 0.1 reshape.244
  8.2 0.1 fusion.14
  8.3 0.1 reduce_window_sum.11
  8.4 0.2 select_reduce_fusion
  8.6 0.8 scatter_custom_fusion
  9.3 0.1 all_to_all.12
  9.4 15.6 %all_to_all.19 = s32[32,1,2]{2,1,0:T(1,128)S(1)} all-to-all(s32[32,1,2]{2,1,0:T(1,128)S(1)} %bitcast.90), channel_id=1, replica_groups=mesh['aux'=4,'pair'=32] {'pair'}, dimensions={0} | all-to-all | bytes 512 | tf_op jit(solution)/shard_map/all_to_all | solution.py:27
  25.0 0.1 copy.59
  25.1 0.1 copy.62
  25.2 0.1 copy.60
  25.3 0.1 copy.63
  25.4 0.1 reshape.269
  25.5 9.8 %gather_fusion = bf16[64,256,512]{2,1,0:T(8,128)(2,1)} fusion(bf16[16,256,512]{2,1,0:T(8,128)(2,1)} %param.8, s32[1024]{0:T(1024)S(1)} %pad_clamp_fusion.3), kind=kCustom, calls=%fused_computation.2 | custom fusion | bytes 33554688 | tf_op jit(solution)/shard_map/jit(_take)/gather | solution.py:32
  35.3 14.3 %select_select_fusion = bf16[32,2,256,512]{3,2,1,0:T(8,128)(2,1)} fusion(bf16[32,2,256,512]{3,2,1,0:T(8,128)(2,1)} %bitcast.81, pred[32,2]{1,0:T(8,128)(4,1)S(1)} %copy.62, pred[32,2]{1,0:T(8,128)(4,1)S(1)} %copy.60), kind=kLoop, calls=%fused_computation.9 | loop fusion | flops 16777216 | bytes 33554560 | tf_op jit(solution)/shard_map/jit(_where)/select_n | solution.py:33
  49.6 5.2 all-to-all-start.1
  54.8 0.2 all-reduce.2.cloned.1.call-start
  55.0 213.0 %all-to-all-done.1 = bf16[32,2,256,512]{3,2,1,0:T(8,128)(2,1)} async-done(((bf16[32,2,256,512]{3,2,1,0:T(8,128)(2,1)}), bf16[32,2,256,512]{3,2,1,0:T(8,128)(2,1)}, u32[]{:S(2)}, u32[]{:S(2)}) %all-to-all-start.1) | async-done | bytes 16777248 | tf_op jit(solution)/shard_map/all_to_all | solution.py:35
  268.0 13.3 %gather_fusion.1 = bf16[62,256,512]{2,1,0:T(8,128)(2,1)} fusion(bf16[64,256,512]{2,1,0:T(8,128)(2,1)} %bitcast.6, s32[1024]{0:T(1024)S(1)} %pad_clamp_fusion.2), kind=kCustom, calls=%fused_computation.3 | custom fusion | bytes 32506104 | tf_op jit(solution)/shard_map/jit(_take)/gather | solution.py:42
  281.3 11.8 %fusion.7 = bf16[62,512,128]{2,1,0:T(8,128)(2,1)} fusion(bf16[62,256,128]{2,1,0:T(8,128)(2,1)} %bitcast.83, bf16[62,256,512]{2,1,0:T(8,128)(2,1)} %gather_fusion.1, pred[62]{0:T(512)(128)(4,1)S(1)} %compare_and_fusion), kind=kOutput, calls=%fused_computation.16 | convolution fusion | flops 2092564480 | bytes 28442686 | tf_op jit(solution)/shard_map/hdp,hdq->hpq/dot_general | solution.py:43
  293.1 6.0 fusion.11
  299.1 0.0 all-reduce.2.cloned.1.call-update
  299.1 0.0 copy-done.3
  299.2 0.7 gather_fusion.3
  299.9 0.7 gather_fusion.2
  300.6 0.1 iota_compare_fusion.1
  300.7 52.8 %all-reduce.2.cloned.1.call-done = f32[31,128,128]{2,1,0:T(8,128)} async-done(((f32[31,128,128]{2,1,0:T(8,128)}), f32[31,128,128]{2,1,0:T(8,128)}) %all-reduce.2.cloned.1.call-update) | async-done | bytes 2031632 | tf_op jit(solution)/shard_map/psum | solution.py:50
  353.5 2.3 copy.67
  355.8 2.7 broadcast_multiply_fusion
  358.5 2.9 copy.68
  361.4 4.0 fusion.13
  365.3 5.5 convert_bitcast_fusion.1
  370.8 3.2 convert_bitcast_fusion.2
  374.0 4.1 pad_maximum_fusion
  378.2 4.3 copy.71
  382.4 11.3 %convert_bitcast_fusion = bf16[62,256,512]{1,2,0:T(8,128)(2,1)} fusion(bf16[62,128,512]{2,1,0:T(8,128)(2,1)} %bitcast.82, bf16[62,256,128]{2,1,0:T(8,128)(2,1)} %bitcast.84), kind=kOutput, calls=%fused_computation.10 | convolution fusion | flops 2088501248 | bytes 28442624 | tf_op jit(solution)/shard_map/hdp,hpq->hdq/dot_general | solution.py:67
  393.7 21.9 %copy.73 = bf16[62,256,512]{2,1,0:T(8,128)(2,1)} copy(bf16[62,256,512]{1,2,0:T(8,128)(2,1)} %convert_bitcast_fusion) | data formatting | bytes 32505856 | tf_op jit(solution)/shard_map/convert_element_type | solution.py:69
  415.6 5.9 broadcast.266
  421.5 41.9 %scatter_fusion = bf16[64,256,512]{2,1,0:T(8,128)(2,1)} fusion(bf16[64,256,512]{2,1,0:T(8,128)(2,1)} %broadcast.266, s32[62]{0:T(128)S(1)} %fusion.22, bf16[62,256,512]{2,1,0:T(8,128)(2,1)} %copy.73), kind=kCustom, calls=%fused_computation.5 | custom fusion | bytes 48759032 | tf_op jit(solution)/shard_map/scatter | solution.py:70
  463.4 7.3 %all-to-all-start.2 = ((bf16[32,2,256,512]{3,2,1,0:T(8,128)(2,1)}), bf16[32,2,256,512]{3,2,1,0:T(8,128)(2,1)}, u32[]{:S(2)}, u32[]{:S(2)}) async-start(bf16[32,2,256,512]{3,2,1,0:T(8,128)(2,1)} %bitcast.80), calls=%async_computation.2 | async-start | bytes 33554432 | tf_op jit(solution)/shard_map/all_to_all | solution.py:71
  470.6 0.1 copy.69
  470.7 0.1 gt.19
  470.9 0.5 broadcast_multiply_fusion.1
  471.4 212.5 %all-to-all-done.2 = bf16[32,2,256,512]{3,2,1,0:T(8,128)(2,1)} async-done(((bf16[32,2,256,512]{3,2,1,0:T(8,128)(2,1)}), bf16[32,2,256,512]{3,2,1,0:T(8,128)(2,1)}, u32[]{:S(2)}, u32[]{:S(2)}) %all-to-all-start.2) | async-done | bytes 16777248 | tf_op jit(solution)/shard_map/all_to_all | solution.py:71
  683.9 16.8 %fusion = f32[16,256,512]{2,0,1:T(8,128)S(1)} fusion(s32[64]{0:T(128)S(1)} %reshape.269, pred[64]{0:T(512)(128)(4,1)S(1)} %gt.19, bf16[8,8,256,512]{3,2,1,0:T(8,128)(2,1)} %bitcast.32), kind=kOutput, calls=%fused_computation.6 | convolution fusion | flops 268437504 | bytes 25166144 | tf_op jit(solution)/shard_map/dot_general | solution.py:82
  700.6 8.3 %copy.75 = f32[16,256,512]{2,1,0:T(8,128)} copy(f32[16,256,512]{2,0,1:T(8,128)S(1)} %fusion) | data formatting | bytes 16777216
  (23 shorter events, 0.1 us)
Async XLA Ops:
  7.2 292.0 %copy-start = (f32[512]{0:T(512)S(1)}, f32[512]{0:T(512)}, u32[]{:S(2)}) copy-start(f32[512]{0:T(512)} %param.9) | copy-start | bytes 6148
  49.6 218.4 %all-to-all-start.1 = ((bf16[32,2,256,512]{3,2,1,0:T(8,128)(2,1)}), bf16[32,2,256,512]{3,2,1,0:T(8,128)(2,1)}, u32[]{:S(2)}, u32[]{:S(2)}) async-start(bf16[32,2,256,512]{3,2,1,0:T(8,128)(2,1)} %select_select_fusion), calls=%async_computation.1 | async-start | bytes 33554432 | tf_op jit(solution)/shard_map/all_to_all | solution.py:35
  54.8 298.7 %all-reduce.2.cloned.1.call-start = ((), (), s32[]{:S(2)}) async-start(), calls=%async_computation.3 | async-start | bytes 4063232 | tf_op jit(solution)/shard_map/psum | solution.py:50
  293.1 6.0 copy-start.3
  293.1 7.5 %copy-start.4 = (s32[31]{0:T(128)S(1)}, s32[31]{0:T(128)}, u32[]{:S(2)}) copy-start(s32[31]{0:T(128)} %param.11) | copy-start | bytes 376
  293.1 62.7 %copy-start.2 = (f32[31,128]{1,0:T(8,128)S(1)}, f32[31,128]{1,0:T(8,128)}, u32[]{:S(2)}) copy-start(f32[31,128]{1,0:T(8,128)} %param.12) | copy-start | bytes 47620
  361.4 9.5 %slice-start = ((s8[8126464]{0:T(1024)(128)(4,1)}), s8[4194304]{0:T(1024)(128)(4,1)S(1)}, s32[]{:S(2)}) async-start(s8[8126464]{0:T(1024)(128)(4,1)} %bitcast.87), calls=%async_computation.4 | async-start | bytes 8388608
  365.3 5.5 slice-start.1
  463.4 220.5 %all-to-all-start.2 = ((bf16[32,2,256,512]{3,2,1,0:T(8,128)(2,1)}), bf16[32,2,256,512]{3,2,1,0:T(8,128)(2,1)}, u32[]{:S(2)}, u32[]{:S(2)}) async-start(bf16[32,2,256,512]{3,2,1,0:T(8,128)(2,1)} %bitcast.80), calls=%async_computation.2 | async-start | bytes 33554432 | tf_op jit(solution)/shard_map/all_to_all | solution.py:71
  683.8 25.0 %copy-start.1 = (f32[512]{0:T(512)S(1)}, f32[512]{0:T(512)}, u32[]{:S(2)}) copy-start(f32[512]{0:T(512)} %param.9) | copy-start | bytes 6148
Sparse Core Ops, SparseCore 0:
  299.2 54.1 all-reduce.1
where the time goes:
time: 717 us; the launch traced here: 716 us
  waiting for transfers between devices  478 us (67%)
  local copies, waits for them, and re-layouts  114 us (16%)
  matrix products  54.5 us (8%)
  other arithmetic  26.1 us (4%)
  blocking collectives  15.6 us (2%)
  between operations  14.2 us (2%)
  starting transfers between devices  12.6 us (2%)
    all_to_all x1, waiting for transfers between devices, local(): lax.all_to_all(selected.reshape(groups, capacity, width_dom, width_aux),...  213 us
    all_to_all x1, waiting for transfers between devices, local(): lax.all_to_all(term_send.reshape(groups, capacity, width_dom, width_aux),...  212 us
    psum x1, waiting for transfers between devices, local(): coupling = lax.psum(partial_sum, 'aux')  52.8 us
    scatter x1, local copies, waits for them, and re-layouts, local(): jnp.zeros((slots, width_dom, width_aux), jnp.bfloat16).at[slot_of]  41.9 us
    convert_element_type x1, local copies, waits for them, and re-layouts, local(): dom_terms = jnp.einsum('hdp,hpq->hdq', coef_half, gamma, preferred_elemen...  21.9 us
    dot_general x1, matrix products, local(): jnp.dot(occ_hot.astype(jnp.bfloat16), terms.reshape(slots, width_dom * wi...  16.8 us
    all_to_all x1, blocking collectives, local(): lax.all_to_all(request.reshape(groups, capacity), 'pair', split_axis=0, c...  15.6 us
  transfers between devices with their start and end apart: 3, of which 3 were waited for; matrix products, arithmetic and copies ran while one was open for 0% of the time, Pallas kernels for 0%

commit v1 on v0

--- a/solution.py
+++ b/solution.py
@@ -2,6 +2,7 @@
 import jax.numpy as jnp
 from jax import lax
 from jax.sharding import PartitionSpec as P
+from jax.lax import all_gather
 
 
 def local(three_index, fock_diag, pair_occ, pno_count, pno_energy, pno_coef):
@@ -47,7 +48,7 @@
     rows_i = paired[:, 0]
     rows_j = paired[:, 1]
     partial_sum = jnp.einsum("kpq,krq->kpr", rows_i, rows_j, preferred_element_type=jnp.float32)
-    coupling = lax.psum(partial_sum, "aux")
+    coupling = jnp.sum(all_gather(partial_sum, axis_name="aux"), 0)
     fock_i = jnp.take(fock_diag, pair_occ[:, 0])
     fock_j = jnp.take(fock_diag, pair_occ[:, 1])
     denom = pno_energy[:, :, None] + pno_energy[:, None, :] - (fock_i + fock_j)[:, None, None]

time: 717 us -> 745 us (1.039)
  waiting for transfers between devices: 478 us -> 502 us
    all_gather x0 -> x1, waiting for transfers between devices: none -> 76.1 us  [local(): coupling = jnp.sum(all_gather(partial_sum, axis_name='aux'), 0)]
    psum x1 -> x0, waiting for transfers between devices: 52.8 us -> none  [local(): coupling = lax.psum(partial_sum, 'aux')]
    reduce_sum x0 -> x2, other arithmetic: none -> 8.39 us  [the longest x1 4.4 us: local(): coupling = jnp.sum(all_gather(partial_sum, axis_name='aux'), 0)]
where the time goes in v1:
time: 745 us; the launch traced here: 744 us
  waiting for transfers between devices  502 us (67%)
  local copies, waits for them, and re-layouts  114 us (15%)
  matrix products  54.6 us (7%)
  other arithmetic  31 us (4%)
  blocking collectives  15.6 us (2%)
  between operations  14.2 us (2%)
  starting transfers between devices  12.6 us (2%)
    all_to_all x1, waiting for transfers between devices, local(): lax.all_to_all(selected.reshape(groups, capacity, width_dom, width_aux),...  213 us
    all_to_all x1, waiting for transfers between devices, local(): lax.all_to_all(term_send.reshape(groups, capacity, width_dom, width_aux),...  212 us
    all_gather x1, waiting for transfers between devices, local(): coupling = jnp.sum(all_gather(partial_sum, axis_name='aux'), 0)  76.1 us
    scatter x1, local copies, waits for them, and re-layouts, local(): jnp.zeros((slots, width_dom, width_aux), jnp.bfloat16).at[slot_of]  41.9 us
    convert_element_type x1, local copies, waits for them, and re-layouts, local(): dom_terms = jnp.einsum('hdp,hpq->hdq', coef_half, gamma, preferred_elemen...  21.9 us
    dot_general x1, matrix products, local(): jnp.dot(occ_hot.astype(jnp.bfloat16), terms.reshape(slots, width_dom * wi...  16.8 us
    all_to_all x1, blocking collectives, local(): lax.all_to_all(request.reshape(groups, capacity), 'pair', split_axis=0, c...  15.6 us
  transfers between devices with their start and end apart: 3, of which 3 were waited for; matrix products, arithmetic and copies ran while one was open for 0% of the time, Pallas kernels for 0%

profile of v1, /device:TPU:0, one launch (start us, length us, event | category | flops | bytes accessed | tf_op | source)
XLA Modules:
  0.0 743.8 jit_solution(10553124941098850134)
XLA Ops:
  7.2 0.0 copy-start
  7.2 0.8 copy.58
  8.0 0.1 reshape.245
  8.1 0.1 reshape.244
  8.2 0.1 fusion.17
  8.3 0.1 reduce_window_sum.11
  8.4 0.2 select_reduce_fusion
  8.6 0.8 scatter_custom_fusion
  9.3 0.1 all_to_all.12
  9.4 15.6 %all_to_all.19 = s32[32,1,2]{2,1,0:T(1,128)S(1)} all-to-all(s32[32,1,2]{2,1,0:T(1,128)S(1)} %bitcast.91), channel_id=1, replica_groups=mesh['aux'=4,'pair'=32] {'pair'}, dimensions={0} | all-to-all | bytes 512 | tf_op jit(solution)/shard_map/all_to_all | solution.py:28
  25.0 0.1 copy.61
  25.1 0.1 copy.64
  25.2 0.1 copy.62
  25.3 0.1 copy.65
  25.4 0.1 reshape.269
  25.5 9.8 %gather_fusion = bf16[64,256,512]{2,1,0:T(8,128)(2,1)} fusion(bf16[16,256,512]{2,1,0:T(8,128)(2,1)} %param.8, s32[1024]{0:T(1024)S(1)} %pad_clamp_fusion.3), kind=kCustom, calls=%fused_computation.2 | custom fusion | bytes 33554688 | tf_op jit(solution)/shard_map/jit(_take)/gather | solution.py:33
  35.3 14.3 %select_select_fusion = bf16[32,2,256,512]{3,2,1,0:T(8,128)(2,1)} fusion(bf16[32,2,256,512]{3,2,1,0:T(8,128)(2,1)} %bitcast.81, pred[32,2]{1,0:T(8,128)(4,1)S(1)} %copy.64, pred[32,2]{1,0:T(8,128)(4,1)S(1)} %copy.62), kind=kLoop, calls=%fused_computation.9 | loop fusion | flops 16777216 | bytes 33554560 | tf_op jit(solution)/shard_map/jit(_where)/select_n | solution.py:34
  49.6 5.2 all-to-all-start.1
  54.8 0.2 all-gather.3.cloned.1.call-start
  55.0 213.0 %all-to-all-done.1 = bf16[32,2,256,512]{3,2,1,0:T(8,128)(2,1)} async-done(((bf16[32,2,256,512]{3,2,1,0:T(8,128)(2,1)}), bf16[32,2,256,512]{3,2,1,0:T(8,128)(2,1)}, u32[]{:S(2)}, u32[]{:S(2)}) %all-to-all-start.1) | async-done | bytes 16777248 | tf_op jit(solution)/shard_map/all_to_all | solution.py:36
  268.0 13.3 %gather_fusion.1 = bf16[62,256,512]{2,1,0:T(8,128)(2,1)} fusion(bf16[64,256,512]{2,1,0:T(8,128)(2,1)} %bitcast.6, s32[1024]{0:T(1024)S(1)} %pad_clamp_fusion.2), kind=kCustom, calls=%fused_computation.3 | custom fusion | bytes 32506104 | tf_op jit(solution)/shard_map/jit(_take)/gather | solution.py:43
  281.3 11.8 %fusion.7 = bf16[62,512,128]{2,1,0:T(8,128)(2,1)} fusion(bf16[62,256,128]{2,1,0:T(8,128)(2,1)} %bitcast.83, bf16[62,256,512]{2,1,0:T(8,128)(2,1)} %gather_fusion.1, pred[62]{0:T(512)(128)(4,1)S(1)} %compare_and_fusion), kind=kOutput, calls=%fused_computation.16 | convolution fusion | flops 2092564480 | bytes 28442686 | tf_op jit(solution)/shard_map/hdp,hdq->hpq/dot_general | solution.py:44
  293.1 6.1 fusion.11
  299.2 0.0 all-gather.3.cloned.1.call-update
  299.2 0.7 gather_fusion.3
  300.0 0.7 gather_fusion.2
  300.7 0.1 iota_compare_fusion.1
  300.8 76.1 %all-gather.3.cloned.1.call-done = f32[124,128,128]{2,1,0:T(8,128)} async-done(((f32[31,128,128]{2,1,0:T(8,128)}), f32[124,128,128]{2,1,0:T(8,128)}) %all-gather.3.cloned.1.call-update) | async-done | bytes 8126480 | tf_op jit(solution)/shard_map/all_gather | solution.py:51
  376.9 4.4 reduce_sum.31
  381.3 2.1 copy.69
  383.4 3.1 neg.7
  386.5 2.9 copy.70
  389.4 4.0 multiply_reduce_fusion
  393.4 5.4 convert_bitcast_fusion.2
  398.8 3.2 convert_bitcast_fusion.1
  402.1 4.1 pad_maximum_fusion
  406.2 4.3 copy.73
  410.5 11.3 %convert_bitcast_fusion = bf16[62,256,512]{1,2,0:T(8,128)(2,1)} fusion(bf16[62,128,512]{2,1,0:T(8,128)(2,1)} %bitcast.82, bf16[62,256,128]{2,1,0:T(8,128)(2,1)} %bitcast.84), kind=kOutput, calls=%fused_computation.10 | convolution fusion | flops 2088501248 | bytes 28442624 | tf_op jit(solution)/shard_map/hdp,hpq->hdq/dot_general | solution.py:68
  421.8 21.9 %copy.75 = bf16[62,256,512]{2,1,0:T(8,128)(2,1)} copy(bf16[62,256,512]{1,2,0:T(8,128)(2,1)} %convert_bitcast_fusion) | data formatting | bytes 32505856 | tf_op jit(solution)/shard_map/convert_element_type | solution.py:70
  443.6 5.9 broadcast.272
  449.5 41.9 %scatter_fusion = bf16[64,256,512]{2,1,0:T(8,128)(2,1)} fusion(bf16[64,256,512]{2,1,0:T(8,128)(2,1)} %broadcast.272, s32[62]{0:T(128)S(1)} %fusion.25, bf16[62,256,512]{2,1,0:T(8,128)(2,1)} %copy.75), kind=kCustom, calls=%fused_computation.5 | custom fusion | bytes 48759032 | tf_op jit(solution)/shard_map/scatter | solution.py:71
  491.4 7.3 all-to-all-start.2
  498.7 0.1 copy.71
  498.8 0.1 gt.19
  498.9 0.5 broadcast_multiply_fusion
  499.4 212.5 %all-to-all-done.2 = bf16[32,2,256,512]{3,2,1,0:T(8,128)(2,1)} async-done(((bf16[32,2,256,512]{3,2,1,0:T(8,128)(2,1)}), bf16[32,2,256,512]{3,2,1,0:T(8,128)(2,1)}, u32[]{:S(2)}, u32[]{:S(2)}) %all-to-all-start.2) | async-done | bytes 16777248 | tf_op jit(solution)/shard_map/all_to_all | solution.py:72
  711.9 16.8 %fusion = f32[16,256,512]{2,0,1:T(8,128)S(1)} fusion(s32[64]{0:T(128)S(1)} %reshape.269, pred[64]{0:T(512)(128)(4,1)S(1)} %gt.19, bf16[8,8,256,512]{3,2,1,0:T(8,128)(2,1)} %bitcast.33), kind=kOutput, calls=%fused_computation.6 | convolution fusion | flops 268437504 | bytes 25166144 | tf_op jit(solution)/shard_map/dot_general | solution.py:83
  728.7 8.3 %copy.77 = f32[16,256,512]{2,1,0:T(8,128)} copy(f32[16,256,512]{2,0,1:T(8,128)S(1)} %fusion) | data formatting | bytes 16777216
  (24 shorter events, 0.1 us)
Async XLA Ops:
  7.2 292.1 %copy-start = (f32[512]{0:T(512)S(1)}, f32[512]{0:T(512)}, u32[]{:S(2)}) copy-start(f32[512]{0:T(512)} %param.9) | copy-start | bytes 6148
  49.6 218.4 %all-to-all-start.1 = ((bf16[32,2,256,512]{3,2,1,0:T(8,128)(2,1)}), bf16[32,2,256,512]{3,2,1,0:T(8,128)(2,1)}, u32[]{:S(2)}, u32[]{:S(2)}) async-start(bf16[32,2,256,512]{3,2,1,0:T(8,128)(2,1)} %select_select_fusion), calls=%async_computation.1 | async-start | bytes 33554432 | tf_op jit(solution)/shard_map/all_to_all | solution.py:36
  54.8 322.1 %all-gather.3.cloned.1.call-start = ((), (), s32[]{:S(2)}) async-start(), calls=%async_computation.3 | async-start | bytes 10158080 | tf_op jit(solution)/shard_map/all_gather | solution.py:51
  293.1 6.1 copy-start.3
  293.1 7.6 %copy-start.4 = (s32[31]{0:T(128)S(1)}, s32[31]{0:T(128)}, u32[]{:S(2)}) copy-start(s32[31]{0:T(128)} %param.11) | copy-start | bytes 376
  381.3 8.1 %copy-start.2 = (f32[31,128]{1,0:T(8,128)S(1)}, f32[31,128]{1,0:T(8,128)}, u32[]{:S(2)}) copy-start(f32[31,128]{1,0:T(8,128)} %param.12) | copy-start | bytes 47620
  389.4 9.4 %slice-start = ((s8[8126464]{0:T(1024)(128)(4,1)}), s8[4194304]{0:T(1024)(128)(4,1)S(1)}, s32[]{:S(2)}) async-start(s8[8126464]{0:T(1024)(128)(4,1)} %bitcast.88), calls=%async_computation.4 | async-start | bytes 8388608
  393.4 5.4 slice-start.1
  491.4 220.5 %all-to-all-start.2 = ((bf16[32,2,256,512]{3,2,1,0:T(8,128)(2,1)}), bf16[32,2,256,512]{3,2,1,0:T(8,128)(2,1)}, u32[]{:S(2)}, u32[]{:S(2)}) async-start(bf16[32,2,256,512]{3,2,1,0:T(8,128)(2,1)} %bitcast.80), calls=%async_computation.2 | async-start | bytes 33554432 | tf_op jit(solution)/shard_map/all_to_all | solution.py:72
  711.9 25.0 %copy-start.1 = (f32[512]{0:T(512)S(1)}, f32[512]{0:T(512)}, u32[]{:S(2)}) copy-start(f32[512]{0:T(512)} %param.9) | copy-start | bytes 6148
Sparse Core Ops, SparseCore 0:
  299.3 77.5 all-gather.2
